TPU v7x, 32 devices: a whole 2x2x4 slice. The times are simulated.
32 devices in a mesh: lines: 2 (over x), col: 16 (over z, y, core).
Axes of the slice: x: 2, y: 2, z: 4, core: 2. Of those that a mesh axis runs over, the one named last changes fastest.
Arguments:
- primary: float32 [16, 4, 128, 256], P(None, 'lines', 'col'), parts along dimension 1, may hold values from -6 to 6
- conductivity: float32 [128, 512], P('col', 'lines'), parts along dimension 1, may hold values from 0.1 to 10
- wavenumbers: float32 [16], replicated, may hold values from 0.05 to 1.5
- quadrature: float32 [16], replicated, may hold values from 0.02 to 0.2
- electrodes: int32 [64], P(('lines', 'col')), parts along dimension 0, may hold values from 0 to 127, as said below
- far_pole: int32 [4, 32], P('lines'), parts along dimension 0, may hold values from 0 to 31, as said below
- observed: float32 [4, 32], P('lines'), parts along dimension 0, may hold values from -6 to 6
- prior_adjoint: float32 [16, 4, 128, 256], P(None, 'lines', 'col'), parts along dimension 1, may hold values from -0.012 to 0.012
Outputs:
- predicted: float32 [4, 32], P('lines'), parts along dimension 0
- gradient: float32 [128, 512], P('col', 'lines'), parts along dimension 1
There are 2 independent parts, one for each index of `lines`. A program takes and returns all parts, laid end to end along the dimension named above; an argument that names none is the same for every part. Nothing has to cross between parts.
Inputs may be any that keep to these rules, and one draw needn't show every extreme that they name: electrodes[e] lies in columns 4 e to 4 e + 3. far_pole[s, r] differs from r by 1 to 8.
All inputs are finite; a program needn't handle non-finite values.
Results may differ from a plain program's by a relative error of at most 0.0003.
Values sent between devices are 32-bit elements; how exact they have to be, the bound alone decides.
A program may use at most 64 MiB of HBM per device.

v0:
```python
import jax
import jax.numpy as jnp
from jax import lax
from jax.sharding import PartitionSpec as P

ITERS = 2


def padded_2(block, sides, width):
    for axis, dim in sides:
        count = lax.axis_size(axis)
        forward = [(i, i + 1) for i in range(count - 1)]
        backward = [(target, source) for source, target in forward]
        low = lax.ppermute(
            lax.slice_in_dim(block, block.shape[dim] - width, None, axis=dim), axis, forward
        )
        high = lax.ppermute(lax.slice_in_dim(block, 0, width, axis=dim), axis, backward)
        block = jnp.concatenate([low, block, high], axis=dim)
    return block


def shifted(value, axis, steps):
    count = lax.axis_size(axis)
    initial, last = (max(0, -steps), min(count, count - steps))
    return lax.ppermute(value, axis, [(source, source + steps) for source in range(initial, last)])


def coefficients(sigma_wide):
    center = sigma_wide[1:-1]
    west_face = 0.5 * (center + sigma_wide[:-2])
    east_face = 0.5 * (center + sigma_wide[2:])
    below_sigma = jnp.concatenate([center[:, 1:], jnp.zeros_like(center[:, :1])], axis=1)
    lower_face = 0.5 * (center + below_sigma)
    above_sigma = jnp.concatenate([jnp.zeros_like(center[:, :1]), center[:, :-1]], axis=1)
    upper_face = 0.5 * (center + above_sigma)
    top_row = jnp.arange(center.shape[1]) == 0
    upper_face = jnp.where(top_row[None, :], 0.0, upper_face)
    return (west_face, east_face, lower_face, upper_face, center)


def stencil(field_wide, faces_set, mass_scale):
    west_face, east_face, lower_face, upper_face, center = faces_set
    middle = field_wide[..., 1:-1, :]
    below_cells = jnp.concatenate([middle[..., 1:], jnp.zeros_like(middle[..., :1])], axis=-1)
    above_cells = jnp.concatenate([jnp.zeros_like(middle[..., :1]), middle[..., :-1]], axis=-1)
    result = west_face * (middle - field_wide[..., :-2, :]) + east_face * (
        middle - field_wide[..., 2:, :]
    )
    result = result + lower_face * (middle - below_cells) + upper_face * (middle - above_cells)
    return result + mass_scale * center * middle


def local_sum(left_field, right_field):
    return jnp.sum(left_field * right_field, axis=(2, 3))


def squares(residual):
    return lax.psum(local_sum(residual, residual), "col")


def expand(scalars):
    return scalars[:, :, None, None]


def conjugate(source, first_image, operate, start):
    solution = start
    residual = source
    direction = source
    norm_now = squares(residual)
    applied = first_image
    for iteration in range(ITERS):
        if iteration > 0:
            applied = operate(direction)
        step_size = norm_now / lax.psum(local_sum(direction, applied), "col")
        solution = solution + expand(step_size) * direction
        if iteration + 1 < ITERS:
            residual = residual - expand(step_size) * applied
            norm_next = squares(residual)
            direction = residual + expand(norm_next / norm_now) * direction
            norm_now = norm_next
    return solution


def on_device(
    primary, conductivity, wavenumbers, quadrature, electrodes, far_pole, observed, prior_adjoint
):
    columns = conductivity.shape[0]
    depth_cells = conductivity.shape[1]
    device = lax.axis_index("col")
    device_count = lax.axis_size("col")
    offset = device * columns
    wide_sigma = padded_2(conductivity, (("col", 0),), 2)
    positions = offset - 2 + jnp.arange(columns + 4)
    inside = (positions >= 0) & (positions < columns * device_count)
    contrast_wide = jnp.where(inside[:, None], wide_sigma - 1.0, 0.0)
    mass_scale = (wavenumbers * wavenumbers)[:, None, None, None]
    operator_faces = coefficients(wide_sigma[1:-1])

    def operate(state):
        padded = padded_2(state, (("col", 2),), 1)
        return stencil(padded, operator_faces, mass_scale)

    padded_primary = padded_2(primary, (("col", 2),), 1)
    source = -stencil(padded_primary, coefficients(contrast_wide[1:-1]), mass_scale)
    first_image = operate(source)
    secondary = conjugate(source, first_image, operate, jnp.zeros_like(source))
    total_field = primary + secondary
    surface = total_field[:, :, :, 0]
    weighted = jnp.einsum("k,ksc->sc", quadrature, surface, precision=lax.Precision.HIGHEST)
    pick_table = (electrodes[:, None] - offset == jnp.arange(columns)[None, :]).astype(jnp.float32)
    own_potentials = jnp.einsum("sc,ec->se", weighted, pick_table, precision=lax.Precision.HIGHEST)
    potentials = lax.all_gather(own_potentials, "col", axis=1, tiled=True)
    predicted = potentials - jnp.take_along_axis(potentials, far_pole, axis=1)
    misfit = predicted - observed
    own_count = electrodes.shape[0]
    own_ids = device * own_count + jnp.arange(own_count)
    own_misfit = lax.dynamic_slice_in_dim(misfit, device * own_count, own_count, 1)
    far_hits = (far_pole[:, :, None] == own_ids[None, None, :]).astype(jnp.float32)
    returned = jnp.einsum("sr,sre->se", misfit, far_hits, precision=lax.Precision.HIGHEST)
    charge = own_misfit - returned
    charge_cols = jnp.einsum("se,ec->sc", charge, pick_table, precision=lax.Precision.HIGHEST)
    surface_row = (jnp.arange(depth_cells) == 0).astype(jnp.float32)
    adjoint_source = quadrature[:, None, None, None] * charge_cols[None, :, :, None] * surface_row
    adjoint_residual = adjoint_source - operate(prior_adjoint)
    adjoint = conjugate(adjoint_residual, operate(adjoint_residual), operate, prior_adjoint)
    edge_columns = shifted((adjoint[:, :, :1], total_field[:, :, :1]), "col", -1)
    adjoint_next = jnp.concatenate([adjoint[:, :, 1:], edge_columns[0]], axis=2)
    total_next = jnp.concatenate([total_field[:, :, 1:], edge_columns[1]], axis=2)
    adjoint_down = jnp.concatenate([adjoint[..., 1:], jnp.zeros_like(adjoint[..., :1])], axis=-1)
    total_down = jnp.concatenate(
        [total_field[..., 1:], jnp.zeros_like(total_field[..., :1])], axis=-1
    )
    correlation = (adjoint_next - adjoint) * (total_next - total_field)
    correlation = correlation + (adjoint_down - adjoint) * (total_down - total_field)
    correlation = correlation + mass_scale * adjoint * total_field
    gradient = jnp.sum(correlation, axis=(0, 1))
    return (predicted, gradient)


def solution(mesh):
    placed = (
        P(None, "lines", "col", None),
        P("col", "lines"),
        P(),
        P(),
        P(("lines", "col")),
        P("lines", None),
        P("lines", None),
        P(None, "lines", "col", None),
    )
    return jax.shard_map(
        on_device,
        mesh=mesh,
        in_specs=placed,
        out_specs=(P("lines", None), P("col", "lines")),
        check_vma=False,
    )
```

profile of v0, /device:TPU:0, one launch (start us, length us, event | category | flops | bytes accessed | tf_op | source)
XLA Modules:
  0.0 319.4 jit_solution(12586996976462141782)
XLA Ops:
  0.6 0.8 fusion.97
  1.4 1.3 collective-permute-start.1
  2.7 3.0 collective-permute-start
  5.7 1.1 fusion.93
  6.8 1.3 collective-permute-start.3
  8.1 5.1 %collective-permute-start.2 = (f32[16,2,1,256]{3,2,1,0:T(1,128)S(1)}, f32[16,2,1,256]{3,2,1,0:T(1,128)S(1)}, u32[]{:S(2)}, u32[]{:S(2)}) collective-permute-start(f32[16,2,1,256]{3,2,1,0:T(1,128)S(1)} %get-tuple-element.44), channel_id=1, source_target_pairs={{0,1},{1,2},{2,3},{3,4},{4,5},{5,6},{6,7},{7,8},{8,9},{9,10},{10,1... | collective-permute-start | bytes 98312 | tf_op jit(solution)/shard_map/ppermute | solution.py:14
  13.3 1.1 fusion.88
  14.3 1.3 collective-permute-start.9
  18.9 4.3 %collective-permute-start.8 = (f32[16,2,1,256]{3,2,1,0:T(1,128)S(1)}, f32[16,2,1,256]{3,2,1,0:T(1,128)S(1)}, u32[]{:S(2)}, u32[]{:S(2)}) collective-permute-start(f32[16,2,1,256]{3,2,1,0:T(1,128)S(1)} %get-tuple-element.34), channel_id=1, source_target_pairs={{0,1},{1,2},{2,3},{3,4},{4,5},{5,6},{6,7},{7,8},{8,9},{9,10},{10,1... | collective-permute-start | bytes 98312 | tf_op jit(solution)/shard_map/ppermute | solution.py:14
  23.9 1.3 collective-permute-start.5
  25.2 4.3 %collective-permute-start.4 = (f32[16,2,1,256]{3,2,1,0:T(1,128)S(1)}, f32[16,2,1,256]{3,2,1,0:T(1,128)S(1)}, u32[]{:S(2)}, u32[]{:S(2)}) collective-permute-start(f32[16,2,1,256]{3,2,1,0:T(1,128)S(1)} %get-tuple-element.40), channel_id=1, source_target_pairs={{0,1},{1,2},{2,3},{3,4},{4,5},{5,6},{6,7},{7,8},{8,9},{9,10},{10,1... | collective-permute-start | bytes 98312 | tf_op jit(solution)/shard_map/ppermute | solution.py:14
  29.6 0.7 collective-permute-done.4
  30.7 62.1 %all-reduce.19 = (f32[16,2]{1,0:T(8,128)S(1)}, f32[16,2]{1,0:T(8,128)S(1)}) all-reduce(f32[16,2]{1,0:T(8,128)S(1)} %get-tuple-element.13, f32[16,2]{1,0:T(8,128)S(1)} %get-tuple-element.12), channel_id=1, replica_groups=mesh['lines'=2,'col'=16] {'col'}, use_global_device_ids=true, to_apply=%region_1.2 | all-reduce | flops 64 | bytes 512 | tf_op jit(solution)/shard_map/psum | solution.py:58
  93.1 30.0 %psum.58 = f32[16,2]{1,0:T(8,128)S(1)} all-reduce(f32[16,2]{1,0:T(8,128)S(1)} %multiply_reduce_fusion.3), channel_id=1, replica_groups=mesh['lines'=2,'col'=16] {'col'}, use_global_device_ids=true, to_apply=%region_5.6 | all-reduce | flops 32 | bytes 256 | tf_op jit(solution)/shard_map/psum | solution.py:58
  123.3 1.3 collective-permute-start.7
  124.6 3.0 collective-permute-start.6
  127.8 0.7 collective-permute-done.6
  128.8 31.3 %psum.59 = f32[16,2]{1,0:T(8,128)S(1)} all-reduce(f32[16,2]{1,0:T(8,128)S(1)} %fusion.55), channel_id=1, replica_groups=mesh['lines'=2,'col'=16] {'col'}, use_global_device_ids=true, to_apply=%region_7.8 | all-reduce | flops 32 | bytes 256 | tf_op jit(solution)/shard_map/psum | solution.py:74
  161.4 17.1 %all-gather = f32[16,2,2]{2,1,0:T(2,128)S(1)} all-gather(f32[1,2,2]{2,1,0:T(2,128)S(1)} %convolution_bitcast_fusion), channel_id=1, replica_groups=mesh['lines'=2,'col'=16] {'col'}, dimensions={0}, use_global_device_ids=true | all-gather | bytes 272 | tf_op jit(solution)/shard_map/all_gather | solution.py:112
  178.6 0.9 gather_fusion
  181.6 1.3 collective-permute-start.11
  182.9 3.0 collective-permute-start.10
  186.1 1.3 collective-permute-start.15
  187.8 60.2 %all-reduce.18 = (f32[16,2]{1,0:T(8,128)S(1)}, f32[16,2]{1,0:T(8,128)S(1)}) all-reduce(f32[16,2]{1,0:T(8,128)S(1)} %get-tuple-element.11, f32[16,2]{1,0:T(8,128)S(1)} %get-tuple-element.10), channel_id=1, replica_groups=mesh['lines'=2,'col'=16] {'col'}, use_global_device_ids=true, to_apply=%region_9.10 | all-reduce | flops 64 | bytes 512 | tf_op jit(solution)/shard_map/psum | solution.py:58
  248.3 30.0 %psum.62 = f32[16,2]{1,0:T(8,128)S(1)} all-reduce(f32[16,2]{1,0:T(8,128)S(1)} %multiply_reduce_fusion), channel_id=1, replica_groups=mesh['lines'=2,'col'=16] {'col'}, use_global_device_ids=true, to_apply=%region_13.14 | all-reduce | flops 32 | bytes 256 | tf_op jit(solution)/shard_map/psum | solution.py:58
  278.5 1.3 collective-permute-start.13
  279.8 3.0 collective-permute-start.12
  283.0 0.7 collective-permute-done.12
  284.0 31.3 %psum.63 = f32[16,2]{1,0:T(8,128)S(1)} all-reduce(f32[16,2]{1,0:T(8,128)S(1)} %fusion.56), channel_id=1, replica_groups=mesh['lines'=2,'col'=16] {'col'}, use_global_device_ids=true, to_apply=%region_15.16 | all-reduce | flops 32 | bytes 256 | tf_op jit(solution)/shard_map/psum | solution.py:74
  315.5 1.3 collective-permute-start.14
  317.2 1.5 collective-permute-done.14
  318.6 0.8 fusion.54
  (86 shorter events, 10.5 us)
Async XLA Ops:
  0.6 15.0 %copy-start = (f32[16,2,8,256]{3,2,1,0:T(8,128)S(1)}, f32[16,2,8,256]{3,2,1,0:T(8,128)}, u32[]{:S(2)}) copy-start(f32[16,2,8,256]{3,2,1,0:T(8,128)} %param.8) | copy-start | bytes 786436
  1.4 17.5 %collective-permute-start.1 = (f32[2,256]{1,0:T(2,128)S(1)}, f32[2,256]{1,0:T(2,128)S(1)}, u32[]{:S(2)}, u32[]{:S(2)}) collective-permute-start(f32[2,256]{1,0:T(2,128)S(1)} %get-tuple-element.62), channel_id=1, source_target_pairs={{1,0},{2,1},{3,2},{4,3},{5,4},{6,5},{7,6},{8,7},{9,8},{10,9},{11,1... | collective-permute-start | bytes 6152 | tf_op jit(solution)/shard_map/ppermute | solution.py:17
  2.7 20.4 %collective-permute-start = (f32[2,256]{1,0:T(2,128)S(1)}, f32[2,256]{1,0:T(2,128)S(1)}, u32[]{:S(2)}, u32[]{:S(2)}) collective-permute-start(f32[2,256]{1,0:T(2,128)S(1)} %get-tuple-element.61), channel_id=1, source_target_pairs={{0,1},{1,2},{2,3},{3,4},{4,5},{5,6},{6,7},{7,8},{8,9},{9,10},{10,1... | collective-permute-start | bytes 6152 | tf_op jit(solution)/shard_map/ppermute | solution.py:14
  6.8 16.7 %collective-permute-start.3 = (f32[16,2,1,256]{3,2,1,0:T(1,128)S(1)}, f32[16,2,1,256]{3,2,1,0:T(1,128)S(1)}, u32[]{:S(2)}, u32[]{:S(2)}) collective-permute-start(f32[16,2,1,256]{3,2,1,0:T(1,128)S(1)} %get-tuple-element.45), channel_id=1, source_target_pairs={{1,0},{2,1},{3,2},{4,3},{5,4},{6,5},{7,6},{8,7},{9,8},{10,9},{11,1... | collective-permute-start | bytes 98312 | tf_op jit(solution)/shard_map/ppermute | solution.py:17
  8.1 15.4 %collective-permute-start.2 = (f32[16,2,1,256]{3,2,1,0:T(1,128)S(1)}, f32[16,2,1,256]{3,2,1,0:T(1,128)S(1)}, u32[]{:S(2)}, u32[]{:S(2)}) collective-permute-start(f32[16,2,1,256]{3,2,1,0:T(1,128)S(1)} %get-tuple-element.44), channel_id=1, source_target_pairs={{0,1},{1,2},{2,3},{3,4},{4,5},{5,6},{6,7},{7,8},{8,9},{9,10},{10,1... | collective-permute-start | bytes 98312 | tf_op jit(solution)/shard_map/ppermute | solution.py:14
  14.3 166.9 %collective-permute-start.9 = (f32[16,2,1,256]{3,2,1,0:T(1,128)S(1)}, f32[16,2,1,256]{3,2,1,0:T(1,128)S(1)}, u32[]{:S(2)}, u32[]{:S(2)}) collective-permute-start(f32[16,2,1,256]{3,2,1,0:T(1,128)S(1)} %get-tuple-element.35), channel_id=1, source_target_pairs={{1,0},{2,1},{3,2},{4,3},{5,4},{6,5},{7,6},{8,7},{9,8},{10,9},{11,1... | collective-permute-start | bytes 98312 | tf_op jit(solution)/shard_map/ppermute | solution.py:17
  15.7 0.7 copy-start.2
  15.7 1.0 copy-start.1
  16.8 0.7 copy-start.6
  17.5 0.7 copy-start.3
  18.1 0.7 copy-start.7
  18.9 162.3 %collective-permute-start.8 = (f32[16,2,1,256]{3,2,1,0:T(1,128)S(1)}, f32[16,2,1,256]{3,2,1,0:T(1,128)S(1)}, u32[]{:S(2)}, u32[]{:S(2)}) collective-permute-start(f32[16,2,1,256]{3,2,1,0:T(1,128)S(1)} %get-tuple-element.34), channel_id=1, source_target_pairs={{0,1},{1,2},{2,3},{3,4},{4,5},{5,6},{6,7},{7,8},{8,9},{9,10},{10,1... | collective-permute-start | bytes 98312 | tf_op jit(solution)/shard_map/ppermute | solution.py:14
  23.9 5.7 %collective-permute-start.5 = (f32[16,2,1,256]{3,2,1,0:T(1,128)S(1)}, f32[16,2,1,256]{3,2,1,0:T(1,128)S(1)}, u32[]{:S(2)}, u32[]{:S(2)}) collective-permute-start(f32[16,2,1,256]{3,2,1,0:T(1,128)S(1)} %get-tuple-element.41), channel_id=1, source_target_pairs={{1,0},{2,1},{3,2},{4,3},{5,4},{6,5},{7,6},{8,7},{9,8},{10,9},{11,1... | collective-permute-start | bytes 98312 | tf_op jit(solution)/shard_map/ppermute | solution.py:17
  25.2 5.1 %collective-permute-start.4 = (f32[16,2,1,256]{3,2,1,0:T(1,128)S(1)}, f32[16,2,1,256]{3,2,1,0:T(1,128)S(1)}, u32[]{:S(2)}, u32[]{:S(2)}) collective-permute-start(f32[16,2,1,256]{3,2,1,0:T(1,128)S(1)} %get-tuple-element.40), channel_id=1, source_target_pairs={{0,1},{1,2},{2,3},{3,4},{4,5},{5,6},{6,7},{7,8},{8,9},{9,10},{10,1... | collective-permute-start | bytes 98312 | tf_op jit(solution)/shard_map/ppermute | solution.py:14
  123.3 4.5 %collective-permute-start.7 = (f32[16,2,1,256]{3,2,1,0:T(1,128)S(1)}, f32[16,2,1,256]{3,2,1,0:T(1,128)S(1)}, u32[]{:S(2)}, u32[]{:S(2)}) collective-permute-start(f32[16,2,1,256]{3,2,1,0:T(1,128)S(1)} %get-tuple-element.37), channel_id=1, source_target_pairs={{1,0},{2,1},{3,2},{4,3},{5,4},{6,5},{7,6},{8,7},{9,8},{10,9},{11,1... | collective-permute-start | bytes 98312 | tf_op jit(solution)/shard_map/ppermute | solution.py:17
  124.6 3.9 %collective-permute-start.6 = (f32[16,2,1,256]{3,2,1,0:T(1,128)S(1)}, f32[16,2,1,256]{3,2,1,0:T(1,128)S(1)}, u32[]{:S(2)}, u32[]{:S(2)}) collective-permute-start(f32[16,2,1,256]{3,2,1,0:T(1,128)S(1)} %get-tuple-element.36), channel_id=1, source_target_pairs={{0,1},{1,2},{2,3},{3,4},{4,5},{5,6},{6,7},{7,8},{8,9},{9,10},{10,1... | collective-permute-start | bytes 98312 | tf_op jit(solution)/shard_map/ppermute | solution.py:14
  160.3 0.7 copy-start.4
  179.5 0.7 copy-start.5
  181.6 5.8 %collective-permute-start.11 = (f32[16,2,1,256]{3,2,1,0:T(1,128)S(1)}, f32[16,2,1,256]{3,2,1,0:T(1,128)S(1)}, u32[]{:S(2)}, u32[]{:S(2)}) collective-permute-start(f32[16,2,1,256]{3,2,1,0:T(1,128)S(1)} %get-tuple-element.29), channel_id=1, source_target_pairs={{1,0},{2,1},{3,2},{4,3},{5,4},{6,5},{7,6},{8,7},{9,8},{10,9},{11,1... | collective-permute-start | bytes 98312 | tf_op jit(solution)/shard_map/ppermute | solution.py:17
  182.9 4.5 %collective-permute-start.10 = (f32[16,2,1,256]{3,2,1,0:T(1,128)S(1)}, f32[16,2,1,256]{3,2,1,0:T(1,128)S(1)}, u32[]{:S(2)}, u32[]{:S(2)}) collective-permute-start(f32[16,2,1,256]{3,2,1,0:T(1,128)S(1)} %get-tuple-element.28), channel_id=1, source_target_pairs={{0,1},{1,2},{2,3},{3,4},{4,5},{5,6},{6,7},{7,8},{8,9},{9,10},{10,1... | collective-permute-start | bytes 98312 | tf_op jit(solution)/shard_map/ppermute | solution.py:14
  186.1 131.1 %collective-permute-start.15 = (f32[16,2,1,256]{3,2,1,0:T(1,128)S(1)}, f32[16,2,1,256]{3,2,1,0:T(1,128)S(1)}, u32[]{:S(2)}, u32[]{:S(2)}) collective-permute-start(f32[16,2,1,256]{3,2,1,0:T(1,128)S(1)} %slice.268), channel_id=1, source_target_pairs={{1,0},{2,1},{3,2},{4,3},{5,4},{6,5},{7,6},{8,7},{9,8},{10,9},{11,1... | collective-permute-start | bytes 98312 | tf_op jit(solution)/shard_map/ppermute | solution.py:25
  278.5 4.5 %collective-permute-start.13 = (f32[16,2,1,256]{3,2,1,0:T(1,128)S(1)}, f32[16,2,1,256]{3,2,1,0:T(1,128)S(1)}, u32[]{:S(2)}, u32[]{:S(2)}) collective-permute-start(f32[16,2,1,256]{3,2,1,0:T(1,128)S(1)} %get-tuple-element.25), channel_id=1, source_target_pairs={{1,0},{2,1},{3,2},{4,3},{5,4},{6,5},{7,6},{8,7},{9,8},{10,9},{11,1... | collective-permute-start | bytes 98312 | tf_op jit(solution)/shard_map/ppermute | solution.py:17
  279.8 3.9 %collective-permute-start.12 = (f32[16,2,1,256]{3,2,1,0:T(1,128)S(1)}, f32[16,2,1,256]{3,2,1,0:T(1,128)S(1)}, u32[]{:S(2)}, u32[]{:S(2)}) collective-permute-start(f32[16,2,1,256]{3,2,1,0:T(1,128)S(1)} %get-tuple-element.24), channel_id=1, source_target_pairs={{0,1},{1,2},{2,3},{3,4},{4,5},{5,6},{6,7},{7,8},{8,9},{9,10},{10,1... | collective-permute-start | bytes 98312 | tf_op jit(solution)/shard_map/ppermute | solution.py:14
  315.5 3.1 collective-permute-start.14
where the time goes:
time: 320 us; the launch traced here: 319 us
  blocking collectives  262 us (82%)
  starting transfers between devices  37.4 us (12%)
  local copies, waits for them, and re-layouts  9.47 us (3%)
  other arithmetic  4.88 us (2%)
  waiting for transfers between devices  3.56 us (1%)
    psum x4, blocking collectives, squares(): return lax.psum(local_sum(residual, residual), 'col')  182 us
    psum x2, blocking collectives, conjugate(): step_size = norm_now / lax.psum(local_sum(direction, applied), 'col')  62.6 us
    ppermute x7, starting transfers between devices, padded_2(): lax.ppermute(lax.slice_in_dim(block, block.shape[dim] - width, None, axis...  25.8 us
    all_gather x1, blocking collectives, on_device(): potentials = lax.all_gather(own_potentials, 'col', axis=1, tiled=True)  17.1 us
    ppermute x7, starting transfers between devices, padded_2(): lax.ppermute(lax.slice_in_dim(block, 0, width, axis=dim), axis, backward)  9.03 us
  transfers between devices with their start and end apart: 16, of which 4 were waited for; matrix products, arithmetic and copies ran while one was open for 3% of the time, Pallas kernels for 0%

commit v1 on v0

v1 whole, which is shorter than its diff:
```python
import functools

import jax
import jax.numpy as jnp
from jax import lax
from jax.experimental import pallas as pl
from jax.experimental.pallas import tpu as pltpu
from jax.sharding import PartitionSpec as P

HALO = 3
F32 = jnp.float32
MESH = pl.DeviceIdType.MESH


def east_of(v):
    return pltpu.roll(v, v.shape[0] - 1, 0)


def divergence(v, east, lower):
    east_flux = east * (v - east_of(v))
    lower_flux = lower * (v - pltpu.roll(v, v.shape[1] - 1, 1))
    return (east_flux - pltpu.roll(east_flux, 1, 0)) + (lower_flux - pltpu.roll(lower_flux, 1, 1))


def face_set(c):
    lanes = lax.broadcasted_iota(jnp.int32, c.shape, 1)
    bottom = lanes == c.shape[1] - 1
    east = 0.5 * (c + east_of(c))
    lower = jnp.where(bottom, 0.0, 0.5 * (c + pltpu.roll(c, c.shape[1] - 1, 1)))
    return east, lower, jnp.where(bottom, 0.5 * c, 0.0)


def fold(product):
    half = product.shape[1] // 2
    return jnp.sum(product[:, :half] + product[:, half:], axis=0, keepdims=True)


def row_sums(block):
    ones = jnp.ones((8, block.shape[1]), F32)
    return lax.dot_general(
        ones, block, (((1,), (1,)), ((), ())), precision=lax.Precision.HIGHEST, preferred_element_type=F32
    )


def step_weights(m, fields):
    m0 = m
    m1, m2, m3 = (pltpu.roll(m, 128 - j * fields, 1) for j in (1, 2, 3))
    a = m0 / m1
    rr = a * a * m2 - m0
    grown = 1.0 + rr / m0
    curve = grown * grown * m1 - 2.0 * grown * a * m2 + a * a * m3
    later = rr / curve
    return a + later * grown, -later * a


def kernel(
    n, prim_hbm, sig_ref, wav_ref, quad_ref, elec_ref, far_ref, obs_ref, prior_hbm, pred_ref, grad_ref,
    prim, prior, sigw, r0f, w0f, nu, nau, na2u, sums, pay, got, pay2, got2, coef, load_sem, halo_send, halo_recv,
    send1, recv1, send2, recv2,
    pack_pr, pack_pl, pack_ar, pack_al, pack_sr, pack_sl, land_pl, land_pr, land_al, land_ar, land_sl, land_sr,
):
    me = lax.axis_index("col")
    fields, cols, depth = prim_hbm.shape
    waves = wav_ref.shape[0]
    sources = fields // waves
    per = elec_ref.shape[0]
    total_e = n * per

    loads = [
        pltpu.make_async_copy(prim_hbm, prim.at[:, pl.ds(0, cols), :], load_sem.at[0]),
        pltpu.make_async_copy(prior_hbm, prior.at[:, pl.ds(0, cols), :], load_sem.at[1]),
    ]
    for c in loads:
        c.start()

    barrier = pltpu.get_barrier_semaphore()

    def greet(j, carry):
        pl.semaphore_signal(barrier, inc=1, device_id={"col": lax.rem(me + j, n)}, device_id_type=MESH)
        return carry

    lax.fori_loop(1, n, greet, 0)
    sig = sig_ref[...]
    pack_sr[...] = sig[cols - HALO :, :]
    pack_sl[...] = sig[:HALO, :]
    for c in loads:
        c.wait()
    pack_pr[...] = prim[:, cols - HALO : cols, :]
    pack_pl[...] = prim[:, 0:HALO, :]
    pack_ar[...] = prior[:, cols - HALO : cols, :]
    pack_al[...] = prior[:, 0:HALO, :]
    pl.semaphore_wait(barrier, n - 1)

    right, left = lax.rem(me + 1, n), lax.rem(me + n - 1, n)

    def halo_copy(src, dst, index, device):
        return pltpu.make_async_remote_copy(
            src_ref=src, dst_ref=dst, send_sem=halo_send.at[index], recv_sem=halo_recv.at[index],
            device_id={"col": device}, device_id_type=MESH,
        )

    to_right = [
        halo_copy(pack_sr, land_sl, 0, right),
        halo_copy(pack_pr, land_pl, 1, right),
        halo_copy(pack_ar, land_al, 2, right),
    ]
    to_left = [
        halo_copy(pack_sl, land_sr, 3, left),
        halo_copy(pack_pl, land_pr, 4, left),
        halo_copy(pack_al, land_ar, 5, left),
    ]
    has_right, has_left = me < n - 1, me > 0

    for i in range(3):
        @pl.when(has_right)
        def _(i=i):
            to_right[i].start()

        @pl.when(has_left)
        def _(i=i):
            to_left[i].start()

    def arrived(i):
        @pl.when(has_left)
        def _():
            to_right[i].wait_recv()

        @pl.when(has_right)
        def _():
            to_left[i].wait_recv()

    rows = lax.broadcasted_iota(jnp.int32, (8, depth), 0)
    keep_low = (rows < HALO) & has_right
    keep_high = (rows >= 8 - HALO) & has_left
    rows16 = lax.broadcasted_iota(jnp.int32, (16, depth), 0)
    inside_b = (rows16 < 8) | ((rows16 < 8 + HALO) & has_right) | ((rows16 >= 16 - HALO) & has_left)
    inside = jnp.where(inside_b, 1.0, 0.0).astype(F32)
    gap = jnp.zeros((8 - 2 * HALO, depth), F32)

    def outer(low, high):
        tile = jnp.concatenate([low, gap, high], axis=0)
        return jnp.where(keep_low | keep_high, tile, 0.0)

    arrived(0)
    sigw[0:8, :] = sig
    sigw[8:16, :] = outer(land_sr[...], land_sl[...])
    c = sigw[...]
    east, lower, bottom = face_set(c)
    contrast = jnp.where(inside_b, c - 1.0, 0.0)
    c_east, c_lower, c_bottom = face_set(contrast)

    lane8 = lax.broadcasted_iota(jnp.int32, (8, 128), 1)
    row8 = lax.broadcasted_iota(jnp.int32, (8, 128), 0)
    picks = [
        jnp.where((lane8 == 0) & (row8 == elec_ref[e] - me * cols), 1.0, 0.0).astype(F32) for e in range(per)
    ]

    arrived(1)

    def forward(k, carry):
        q = wav_ref[k] * wav_ref[k]
        weight = quad_ref[k]
        diagonal = q * c + bottom
        for s in range(sources):
            ks = k * sources + s
            high = outer(land_pr[ks], land_pl[ks])
            prim[ks, 8:16, :] = high
            v = jnp.concatenate([prim[ks, 0:8, :], high], axis=0)
            r = -(divergence(v, c_east, c_lower) + (q * contrast + c_bottom) * v) * inside
            w = (divergence(r, east, lower) + diagonal * r) * inside
            aw = divergence(w, east, lower) + diagonal * w
            r0f[ks] = r
            w0f[ks] = w
            v8, r8, w8, aw8 = v[:8], r[:8], w[:8], aw[:8]
            for j, product in enumerate((r8 * r8, r8 * w8, w8 * w8, w8 * aw8)):
                sums[0, pl.ds(j * fields + ks, 1), :] = fold(product)
            for e in range(per):
                pick = picks[e] * weight
                for j, field in enumerate((v8, r8, w8)):
                    sums[1 + e, pl.ds(j * fields + ks, 1), :] = jnp.sum(pick * field[:, :128], axis=0, keepdims=True)
        return carry

    lax.fori_loop(0, waves, forward, 0)
    for e in range(per):
        rest = 128 - 3 * fields
        where = jnp.where(
            (lax.broadcasted_iota(jnp.int32, (rest, 128), 0) == 0)
            & (lax.broadcasted_iota(jnp.int32, (rest, 128), 1) == 0),
            elec_ref[e].astype(F32),
            0.0,
        )
        sums[1 + e, 3 * fields :, :] = where
    for g in range(1 + per):
        pay[g : g + 1, :] = row_sums(sums[g])[0:1, :]

    def spread(src, dst, send, recv, j):
        return pltpu.make_async_remote_copy(
            src_ref=src, dst_ref=dst.at[me], send_sem=send.at[j], recv_sem=recv.at[j],
            device_id={"col": lax.rem(me + j, n)}, device_id_type=MESH,
        )

    def collect(src, dst, send, recv, j):
        return pltpu.make_async_remote_copy(
            src_ref=src, dst_ref=dst.at[lax.rem(me + n - j, n)], send_sem=send.at[j], recv_sem=recv.at[j],
            device_id={"col": lax.rem(me + j, n)}, device_id_type=MESH,
        )

    def start_all(src, dst, send, recv):
        def body(j, carry):
            spread(src, dst, send, recv, j).start()
            return carry

        lax.fori_loop(1, n, body, 0)
        dst[me] = src[...]

    def wait_all(src, dst, send, recv):
        def body(j, carry):
            collect(src, dst, send, recv, j).wait_recv()
            return carry

        lax.fori_loop(1, n, body, 0)

    def sent_all(src, dst, send, recv):
        def body(j, carry):
            spread(src, dst, send, recv, j).wait_send()
            return carry

        lax.fori_loop(1, n, body, 0)

    start_all(pay, got, send1, recv1)

    arrived(2)

    def before(k, carry):
        q = wav_ref[k] * wav_ref[k]
        diagonal = q * c + bottom
        for s in range(sources):
            ks = k * sources + s
            high = outer(land_ar[ks], land_al[ks])
            prior[ks, 8:16, :] = high
            v = jnp.concatenate([prior[ks, 0:8, :], high], axis=0)
            r = -(divergence(v, east, lower) + diagonal * v) * inside
            w = (divergence(r, east, lower) + diagonal * r) * inside
            aw = divergence(w, east, lower) + diagonal * w
            nu[ks] = r
            nau[ks] = w
            na2u[ks] = aw[:8, :128]
            half = depth // 2
            r8, w8, aw8 = r[:8, half:], w[:8, half:], aw[:8, half:]
            for j, product in enumerate((r8 * r8, r8 * w8, w8 * w8, w8 * aw8)):
                sums[0, pl.ds(j * fields + ks, 1), :] = jnp.sum(product, axis=0, keepdims=True)
        return carry

    lax.fori_loop(0, waves, before, 0)

    def spread_weights(row, slot):
        at = lax.broadcasted_iota(jnp.int32, (fields, 128), 0) == lax.broadcasted_iota(jnp.int32, (fields, 128), 1)
        column = jnp.sum(jnp.where(at, jnp.broadcast_to(row, (fields, 128)), 0.0), axis=1, keepdims=True)
        coef[slot] = jnp.broadcast_to(column, (fields, depth))

    wait_all(pay, got, send1, recv1)
    m = jnp.sum(got[:, 0, :], axis=0, keepdims=True)
    first, second = step_weights(m, fields)
    lane = lax.broadcasted_iota(jnp.int32, (1, 128), 1)
    scale = jnp.where(
        lane < fields,
        1.0,
        jnp.where(
            lane < 2 * fields,
            pltpu.roll(first, fields, 1),
            jnp.where(lane < 3 * fields, pltpu.roll(second, 2 * fields, 1), 0.0),
        ),
    )
    device_ids = lax.broadcasted_iota(jnp.int32, (n, total_e), 0)
    receivers = lax.broadcasted_iota(jnp.int32, (n, total_e), 1)
    marks = [got[:, 1 + e, :] for e in range(per)]
    lane_n = lax.broadcasted_iota(jnp.int32, (n, 128), 1)
    places = [jnp.sum(jnp.where(lane_n == 3 * fields, marks[e], 0.0), axis=1, keepdims=True) for e in range(per)]
    columns_here = lax.broadcasted_iota(jnp.int32, (n, 128), 1)
    column_of = (me * cols + jnp.where(columns_here < 8 + HALO, columns_here, columns_here - 16)).astype(F32)
    hits = [places[e] == column_of for e in range(per)]
    charges = []
    for s in range(sources):
        scale_s = jnp.where(lax.rem(lane, sources) == s, scale, 0.0)
        pair = []
        row = jnp.zeros((1, total_e), F32)
        for e in range(per):
            potential = jnp.sum(marks[e] * scale_s, axis=1, keepdims=True)
            own_id = device_ids * per + e
            near = jnp.where(receivers == own_id, 1.0, 0.0)
            far = jnp.where(jnp.broadcast_to(far_ref[s : s + 1, :], (n, total_e)) == own_id, 1.0, 0.0)
            pair.append(near - far)
            row = row + jnp.sum(potential * (near - far), axis=0, keepdims=True)
        pred_ref[s : s + 1, :] = row
        misfit = row - obs_ref[s : s + 1, :]
        spots = jnp.zeros((1, 128), F32)
        for e in range(per):
            charge = jnp.sum(pair[e] * misfit, axis=1, keepdims=True)
            spots = spots + jnp.sum(jnp.where(hits[e], charge, 0.0), axis=0, keepdims=True)
        charges.append(spots)

    row16 = lax.broadcasted_iota(jnp.int32, (16, 128), 0)
    lane16 = lax.broadcasted_iota(jnp.int32, (16, 128), 1)
    inside0 = inside[:, :128]
    c0 = c[:, :128]
    east0 = east[:, :128]
    lower0 = jnp.where(lane16 < 127, lower[:, :128], 0.0)
    impulse = []
    for s in range(sources):
        column = jnp.sum(
            jnp.where(lane16 == row16, jnp.broadcast_to(charges[s], (16, 128)), 0.0), axis=1, keepdims=True
        )
        g = jnp.where(lane16 == 0, column, 0.0) * inside0
        b = divergence(g, east0, lower0) * inside0
        d = c0 * g
        impulse.append((g, b, d, divergence(b, east0, lower0), divergence(d, east0, lower0) + c0 * b, c0 * d))

    def after(k, carry):
        q = wav_ref[k] * wav_ref[k]
        weight = quad_ref[k]
        for s in range(sources):
            ks = k * sources + s
            g, b, d, b2, x, d2 = impulse[s]
            r = weight * g + nu[ks, :, 0:128]
            w = weight * (b + q * d) + nau[ks, :, 0:128]
            nu[ks, :, 0:128] = r
            nau[ks, :, 0:128] = w
            aw8 = weight * (b2[:8] + q * (x[:8] + q * d2[:8])) + na2u[ks]
            r8, w8 = r[:8], w[:8]
            for j, product in enumerate((r8 * r8, r8 * w8, w8 * w8, w8 * aw8)):
                at = pl.ds(j * fields + ks, 1)
                sums[0, at, :] = sums[0, at, :] + jnp.sum(product, axis=0, keepdims=True)
        return carry

    lax.fori_loop(0, waves, after, 0)
    pay2[...] = row_sums(sums[0])[0:1, :]
    start_all(pay2, got2, send2, recv2)

    spread_weights(first, 0)
    spread_weights(second, 1)

    def totals(ks, carry):
        prim[ks] = prim[ks] + coef[0, pl.ds(ks, 1), :] * r0f[ks] + coef[1, pl.ds(ks, 1), :] * w0f[ks]
        return carry

    lax.fori_loop(0, fields, totals, 0)
    sent_all(pay, got, send1, recv1)
    for i in range(3):
        @pl.when(has_right)
        def _(i=i):
            to_right[i].wait_send()

        @pl.when(has_left)
        def _(i=i):
            to_left[i].wait_send()

    wait_all(pay2, got2, send2, recv2)
    first, second = step_weights(jnp.sum(got2[:, 0, :], axis=0, keepdims=True), fields)
    spread_weights(first, 0)
    spread_weights(second, 1)
    last = lax.broadcasted_iota(jnp.int32, (8, depth), 1) == depth - 1

    def correlate(k, total):
        q = wav_ref[k] * wav_ref[k]
        for s in range(sources):
            ks = k * sources + s
            t = prim[ks]
            a = prior[ks] + coef[0, pl.ds(ks, 1), :] * nu[ks] + coef[1, pl.ds(ks, 1), :] * nau[ks]
            t_east, a_east = east_of(t)[:8], east_of(a)[:8]
            t, a = t[:8], a[:8]
            t_down = jnp.where(last, 0.0, pltpu.roll(t, depth - 1, 1))
            a_down = jnp.where(last, 0.0, pltpu.roll(a, depth - 1, 1))
            total = total + ((a_east - a) * (t_east - t) + (a_down - a) * (t_down - t) + q * a * t)
        return total

    grad_ref[...] = lax.fori_loop(0, waves, correlate, jnp.zeros((8, depth), F32))
    sent_all(pay2, got2, send2, recv2)


def on_device(n, primary, conductivity, wavenumbers, quadrature, electrodes, far_pole, observed, prior_adjoint):
    waves, sources, cols, depth = primary.shape
    fields = waves * sources
    per = electrodes.shape[0]
    vmem, smem = (pl.BlockSpec(memory_space=m) for m in (pltpu.VMEM, pltpu.SMEM))
    anywhere = pl.BlockSpec(memory_space=pl.ANY)
    wide = pltpu.VMEM((fields, 16, depth), F32)
    edge = pltpu.VMEM((fields, HALO, depth), F32)
    sigma_edge = pltpu.VMEM((HALO, depth), F32)
    dma = pltpu.SemaphoreType.DMA
    return pl.pallas_call(
        functools.partial(kernel, n),
        out_shape=(
            jax.ShapeDtypeStruct(observed.shape, F32),
            jax.ShapeDtypeStruct(conductivity.shape, F32),
        ),
        in_specs=[anywhere, vmem, smem, smem, smem, vmem, vmem, anywhere],
        out_specs=(vmem, vmem),
        scratch_shapes=[
            wide, wide, pltpu.VMEM((16, depth), F32), wide, wide, wide, wide,
            pltpu.VMEM((fields, 8, 128), F32),
            pltpu.VMEM((1 + per, 128, 128), F32),
            pltpu.VMEM((1 + per, 128), F32), pltpu.VMEM((n, 1 + per, 128), F32),
            pltpu.VMEM((1, 128), F32), pltpu.VMEM((n, 1, 128), F32),
            pltpu.VMEM((2, fields, depth), F32),
            dma((2,)), dma((6,)), dma((6,)), dma((n,)), dma((n,)), dma((n,)), dma((n,)),
            edge, edge, edge, edge, sigma_edge, sigma_edge, edge, edge, edge, edge, sigma_edge, sigma_edge,
        ],
        compiler_params=pltpu.CompilerParams(
            collective_id=0, has_side_effects=True, vmem_limit_bytes=32 * 1024 * 1024
        ),
    )(
        primary.reshape(fields, cols, depth), conductivity, wavenumbers, quadrature, electrodes, far_pole, observed,
        prior_adjoint.reshape(fields, cols, depth),
    )


def solution(mesh):
    placed = (
        P(None, "lines", "col", None), P("col", "lines"), P(), P(), P(("lines", "col")),
        P("lines", None), P("lines", None), P(None, "lines", "col", None),
    )
    return jax.shard_map(
        functools.partial(on_device, mesh.shape["col"]),
        mesh=mesh, in_specs=placed, out_specs=(P("lines", None), P("col", "lines")), check_vma=False,
    )
```

time: 320 us -> 39.5 us (0.12)
  blocking collectives: 262 us -> 0 us
  starting transfers between devices: 37.4 us -> 0 us
  Pallas kernels: 0 us -> 34.1 us
  local copies, waits for them, and re-layouts: 9.47 us -> 4.45 us
  other arithmetic: 4.88 us -> 0 us
  waiting for transfers between devices: 3.56 us -> 0 us
    psum x6 -> x0, blocking collectives: 245 us -> none  [the longest x4 182 us: squares(): return lax.psum(local_sum(residual, residual), 'col')]
    ppermute x16 -> x0, starting transfers between devices: 37.4 us -> none  [the longest x7 25.8 us: padded_2(): lax.ppermute(lax.slice_in_dim(block, block.shape[dim] - width, None, axis...]
    pallas_call x0 -> x1, Pallas kernels: none -> 34.1 us  [on_device(): pl.pallas_call(functools.partial(kernel, n), out_shape=(jax.ShapeDtypeStr...]
    all_gather x1 -> x0, blocking collectives: 17.1 us -> none  [on_device(): potentials = lax.all_gather(own_potentials, 'col', axis=1, tiled=True)]
    slice x23 -> x0, local copies, waits for them, and re-layouts: 4.58 us -> none  [the longest x7 3.11 us: padded_2(): lax.slice_in_dim(block, block.shape[dim] - width, None, axis=dim)]
    ppermute x16 -> x0, waiting for transfers between devices: 3.56 us -> none  [the longest x7 2.08 us: padded_2(): lax.ppermute(lax.slice_in_dim(block, block.shape[dim] - width, None, axis...]
  transfers between devices with their start and end apart: 16 -> 0, of which waited for: 4 -> 0; matrix products, arithmetic and copies ran while one was open for 3% -> 0% of each run, Pallas kernels for 0% -> 0%
where the time goes in v1:
time: 39.5 us; the launch traced here: 39.3 us
  Pallas kernels  34.1 us (86%)
  local copies, waits for them, and re-layouts  4.45 us (11%)
  between operations  0.69 us (2%)
    pallas_call x1, Pallas kernels, on_device(): pl.pallas_call(functools.partial(kernel, n), out_shape=(jax.ShapeDtypeStr...  34.1 us
    unnamed x18, local copies, waits for them, and re-layouts  4.45 us

profile of v1, /device:TPU:0, one launch (start us, length us, event | category | flops | bytes accessed | tf_op | source)
XLA Modules:
  0.0 39.3 jit_solution(17307877134774323728)
XLA Ops:
  0.6 0.0 copy-start.4
  0.6 0.0 copy-start.6
  0.7 0.0 copy-start.7
  0.7 0.0 copy-start.3
  0.7 0.0 copy-start.5
  0.7 0.6 %copy-done.4 = f32[2,32]{1,0:T(2,128)S(1)} copy-done((f32[2,32]{1,0:T(2,128)S(1)}, f32[2,32]{1,0:T(2,128)}, u32[]{:S(2)}) %copy-start.4) | copy-done | bytes 280
  1.3 0.0 copy-done.6
  1.3 0.0 copy-done.7
  1.3 0.0 copy-done.3
  1.4 0.0 copy-done.5
  1.4 0.0 copy-start
  1.4 0.9 %copy-done = f32[16,2,8,256]{3,2,1,0:T(8,128)S(1)} copy-done((f32[16,2,8,256]{3,2,1,0:T(8,128)S(1)}, f32[16,2,8,256]{3,2,1,0:T(8,128)}, u32[]{:S(2)}) %copy-start) | copy-done | bytes 262168
  2.3 0.0 copy-start.1
  2.3 0.9 %copy-done.1 = f32[16,2,8,256]{3,2,1,0:T(8,128)S(1)} copy-done((f32[16,2,8,256]{3,2,1,0:T(8,128)S(1)}, f32[16,2,8,256]{3,2,1,0:T(8,128)}, u32[]{:S(2)}) %copy-start.1) | copy-done | bytes 262168
  3.3 0.0 copy-start.2
  3.3 0.7 %copy-done.2 = f32[8,256]{1,0:T(8,128)S(1)} copy-done((f32[8,256]{1,0:T(8,128)S(1)}, f32[8,256]{1,0:T(8,128)}, u32[]{:S(2)}) %copy-start.2) | copy-done | bytes 8216
  4.0 34.1 %shard_map.95 = (f32[2,32]{1,0:T(2,128)S(1)}, f32[8,256]{1,0:T(8,128)S(1)}) custom-call(f32[32,8,256]{2,1,0:T(8,128)S(1)} %bitcast.2, f32[8,256]{1,0:T(8,128)S(1)} %copy-done.2, f32[16]{0:T(128)S(1)} %copy-done.5, f32[16]{0:T(128)S(1)} %copy-done.6, s32[2]{0:T(128)S(1)} %copy-done.7, s32[2,32]{1,0:T(2,128)S(1)} %copy-done.3, f32[2,32]{1,0:T(2,128)S(1)} %copy-done.4, ...), custom_call_target="tpu_custom_call" | custom-call | tf_op jit(solution)/shard_map/pallas_call | solution.py:390
  38.1 0.6 %copy.12 = f32[2,32]{1,0:T(2,128)} copy(f32[2,32]{1,0:T(2,128)S(1)} %get-tuple-element.4) | data formatting | bytes 512
  38.7 0.6 %copy.13 = f32[8,256]{1,0:T(8,128)} copy(f32[8,256]{1,0:T(8,128)S(1)} %get-tuple-element.5) | data formatting | bytes 16384
Async XLA Ops:
  0.6 0.7 %copy-start.4 = (f32[2,32]{1,0:T(2,128)S(1)}, f32[2,32]{1,0:T(2,128)}, u32[]{:S(2)}) copy-start(f32[2,32]{1,0:T(2,128)} %obs_ref.1) | copy-start | bytes 772
  0.6 0.7 %copy-start.6 = (f32[16]{0:T(128)S(1)}, f32[16]{0:T(128)}, u32[]{:S(2)}) copy-start(f32[16]{0:T(128)} %quad_ref.1) | copy-start | bytes 196
  0.7 0.7 %copy-start.7 = (s32[2]{0:T(128)S(1)}, s32[2]{0:T(128)}, u32[]{:S(2)}) copy-start(s32[2]{0:T(128)} %elec_ref.1) | copy-start | bytes 28
  0.7 0.7 %copy-start.3 = (s32[2,32]{1,0:T(2,128)S(1)}, s32[2,32]{1,0:T(2,128)}, u32[]{:S(2)}) copy-start(s32[2,32]{1,0:T(2,128)} %far_ref.1) | copy-start | bytes 772
  0.7 0.7 %copy-start.5 = (f32[16]{0:T(128)S(1)}, f32[16]{0:T(128)}, u32[]{:S(2)}) copy-start(f32[16]{0:T(128)} %wav_ref.1) | copy-start | bytes 196
  1.4 1.0 %copy-start = (f32[16,2,8,256]{3,2,1,0:T(8,128)S(1)}, f32[16,2,8,256]{3,2,1,0:T(8,128)}, u32[]{:S(2)}) copy-start(f32[16,2,8,256]{3,2,1,0:T(8,128)} %param.8) | copy-start | bytes 786436
  2.3 0.9 %copy-start.1 = (f32[16,2,8,256]{3,2,1,0:T(8,128)S(1)}, f32[16,2,8,256]{3,2,1,0:T(8,128)}, u32[]{:S(2)}) copy-start(f32[16,2,8,256]{3,2,1,0:T(8,128)} %param.15) | copy-start | bytes 786436
  3.3 0.7 %copy-start.2 = (f32[8,256]{1,0:T(8,128)S(1)}, f32[8,256]{1,0:T(8,128)}, u32[]{:S(2)}) copy-start(f32[8,256]{1,0:T(8,128)} %sig_ref.1) | copy-start | bytes 24580

commit v2 on v1

v2 whole, which is shorter than its diff:
```python
import functools

import jax
import jax.numpy as jnp
from jax import lax
from jax.experimental import pallas as pl
from jax.experimental.pallas import tpu as pltpu
from jax.sharding import PartitionSpec as P

LEFT, RIGHT = 2, 3
GROUP = 4
F32 = jnp.float32
MESH = pl.DeviceIdType.MESH


def east_of(v):
    return pltpu.roll(v, v.shape[0] - 1, 0)


def divergence(v, east, lower):
    east_flux = east * (v - east_of(v))
    lower_flux = lower * (v - pltpu.roll(v, v.shape[1] - 1, 1))
    return (east_flux - pltpu.roll(east_flux, 1, 0)) + (lower_flux - pltpu.roll(lower_flux, 1, 1))


def face_set(c):
    lanes = lax.broadcasted_iota(jnp.int32, c.shape, 1)
    bottom = lanes == c.shape[1] - 1
    east = 0.5 * (c + east_of(c))
    lower = jnp.where(bottom, 0.0, 0.5 * (c + pltpu.roll(c, c.shape[1] - 1, 1)))
    return east, lower, jnp.where(bottom, 0.5 * c, 0.0)


def fold(product):
    half = product.shape[1] // 2
    return product[:, :half] + product[:, half:]


def stack_sums(tiles):
    row = lax.broadcasted_iota(jnp.int32, tiles[0].shape, 0)
    low = row < 4
    y = [
        jnp.where(low, tiles[i], tiles[i + 4]) + pltpu.roll(jnp.where(low, tiles[i + 4], tiles[i]), 4, 0)
        for i in range(4)
    ]
    even = (row & 2) == 0
    z = [
        jnp.where(even, y[i] + pltpu.roll(y[i], 6, 0), y[i + 2] + pltpu.roll(y[i + 2], 2, 0)) for i in range(2)
    ]
    return jnp.where((row & 1) == 0, z[0] + pltpu.roll(z[0], 7, 0), z[1] + pltpu.roll(z[1], 1, 0))


def energy(w, east, lower, diagonal):
    across = w - east_of(w)
    down = w - pltpu.roll(w, w.shape[1] - 1, 1)
    return (east * across * across + lower * down * down + diagonal * w * w)[:8]


def row_sums(block):
    ones = jnp.ones((8, block.shape[1]), F32)
    return lax.dot_general(
        ones, block, (((1,), (1,)), ((), ())), precision=lax.Precision.HIGHEST, preferred_element_type=F32
    )


def step_weights(m, sources):
    m0 = m
    m1, m2, m3 = (pltpu.roll(m, 128 - j * sources, 1) for j in (1, 2, 3))
    a = m0 / m1
    rr = a * a * m2 - m0
    grown = 1.0 + rr / m0
    curve = grown * grown * m1 - 2.0 * grown * a * m2 + a * a * m3
    later = rr / curve
    return a + later * grown, -later * a


def kernel(
    n, prim_hbm, sig_hbm, wav_hbm, quad_hbm, elec_hbm, far_hbm, obs_hbm, prior_hbm, pred_ref, grad_ref,
    prim, prior, sigw, wav_ref, quad_ref, elec_ref, far_ref, obs_ref,
    r0f, w0f, nu, nau, sums, pay, got, pay2, got2, coef, load_sem,
    send_r, recv_r, send_l, recv_l, send1, recv1, send2, recv2,
    pack_pr, pack_pl, pack_ar, pack_al, pack_sr, pack_sl, land_pl, land_pr, land_al, land_ar, land_sl, land_sr,
):
    me = lax.axis_index("col")
    fields, cols, depth = prim_hbm.shape
    waves = wav_hbm.shape[0]
    sources = fields // waves
    per = elec_hbm.shape[0]
    total_e = n * per
    chunks = waves // GROUP
    span = GROUP * sources

    loads = [
        pltpu.make_async_copy(src, dst, load_sem.at[i])
        for i, (src, dst) in enumerate((
            (sig_hbm, sigw.at[pl.ds(0, cols), :]),
            (prim_hbm, prim.at[:, pl.ds(0, cols), :]),
            (prior_hbm, prior.at[:, pl.ds(0, cols), :]),
            (wav_hbm, wav_ref), (quad_hbm, quad_ref), (elec_hbm, elec_ref), (far_hbm, far_ref), (obs_hbm, obs_ref),
        ))
    ]
    for copy in loads:
        copy.start()

    barrier = pltpu.get_barrier_semaphore()

    def greet(j, carry):
        pl.semaphore_signal(barrier, inc=1, device_id={"col": lax.rem(me + j, n)}, device_id_type=MESH)
        return carry

    lax.fori_loop(1, n, greet, 0, unroll=n <= 16)
    loads[0].wait()
    sig = sigw[0:8, :]
    pack_sr[...] = sig[cols - LEFT :, :]
    pack_sl[...] = sig[:RIGHT, :]
    loads[1].wait()
    pack_pr[...] = prim[:, cols - LEFT : cols, :]
    pack_pl[...] = prim[:, 0:RIGHT, :]
    pl.semaphore_wait(barrier, n - 1)

    right, left = lax.rem(me + 1, n), lax.rem(me + n - 1, n)
    has_right, has_left = me < n - 1, me > 0

    def both(index, rightward, leftward):
        return (
            pltpu.make_async_remote_copy(
                src_ref=rightward[0], dst_ref=rightward[1], send_sem=send_r.at[index], recv_sem=recv_r.at[index],
                device_id={"col": right}, device_id_type=MESH,
            ),
            pltpu.make_async_remote_copy(
                src_ref=leftward[0], dst_ref=leftward[1], send_sem=send_l.at[index], recv_sem=recv_l.at[index],
                device_id={"col": left}, device_id_type=MESH,
            ),
        )

    def sigma_halo():
        return both(2 * chunks, (pack_sr, land_sl), (pack_sl, land_sr))

    def prim_halo(g):
        at = pl.ds(g * span, span)
        return both(g, (pack_pr.at[at], land_pl.at[at]), (pack_pl.at[at], land_pr.at[at]))

    def prior_halo(g):
        at = pl.ds(g * span, span)
        return both(chunks + g, (pack_ar.at[at], land_al.at[at]), (pack_al.at[at], land_ar.at[at]))

    def start_both(pair):
        @pl.when(has_right)
        def _():
            pair[0].start()

        @pl.when(has_left)
        def _():
            pair[1].start()

    def arrived(pair):
        @pl.when(has_left)
        def _():
            pair[0].wait_recv()

        @pl.when(has_right)
        def _():
            pair[1].wait_recv()

    def sent(pair):
        @pl.when(has_right)
        def _():
            pair[0].wait_send()

        @pl.when(has_left)
        def _():
            pair[1].wait_send()

    start_both(sigma_halo())
    for g in range(chunks):
        start_both(prim_halo(g))
    loads[2].wait()
    pack_ar[...] = prior[:, cols - LEFT : cols, :]
    pack_al[...] = prior[:, 0:RIGHT, :]
    for g in range(chunks):
        start_both(prior_halo(g))
    for copy in loads[3:]:
        copy.wait()

    rows = lax.broadcasted_iota(jnp.int32, (8, depth), 0)
    keep = ((rows < RIGHT) & has_right) | ((rows >= 8 - LEFT) & has_left)
    inside8 = jnp.where(keep, 1.0, 0.0).astype(F32)
    inside = jnp.concatenate([jnp.ones((8, depth), F32), inside8], axis=0)
    gap = jnp.zeros((8 - LEFT - RIGHT, depth), F32)

    def outer(low, high):
        return jnp.where(keep, jnp.concatenate([low, gap, high], axis=0), 0.0)

    def clip(v):
        return jnp.concatenate([v[:8], v[8:] * inside8[:, : v.shape[1]]], axis=0)

    arrived(sigma_halo())
    sigw[8:16, :] = outer(land_sr[...], land_sl[...])
    c = sigw[...]
    east, lower, bottom = face_set(c)
    contrast = (c - 1.0) * inside
    c_east, c_lower, c_bottom = face_set(contrast)
    rows16 = lax.broadcasted_iota(jnp.int32, (16, depth), 0)
    edge = jnp.where((rows16 == 0) & (me == 0), 0.5 * c, 0.0)

    lane8 = lax.broadcasted_iota(jnp.int32, (8, 128), 1)
    row8 = lax.broadcasted_iota(jnp.int32, (8, 128), 0)
    picks = [
        jnp.where((lane8 == 0) & (row8 == elec_ref[e] - me * cols), 1.0, 0.0).astype(F32) for e in range(per)
    ]

    empty = jnp.zeros((8, 128), F32)

    def forward(g, carry):
        arrived(prim_halo(g))
        for step in range(GROUP):
            k = g * GROUP + step
            q = wav_ref[k] * wav_ref[k]
            weight = quad_ref[k]
            diagonal = q * c + bottom
            source_diagonal = q * contrast + c_bottom
            moments, spots = {}, {}
            for s in range(sources):
                ks = k * sources + s
                high = outer(land_pr[ks], land_pl[ks])
                prim[ks, 8:16, :] = high
                v = jnp.concatenate([prim[ks, 0:8, :], high], axis=0)
                r = clip(-(divergence(v, c_east, c_lower) + source_diagonal * v))
                w = clip(divergence(r, east, lower) + diagonal * r)
                r0f[ks] = r
                w0f[ks] = w
                r8, w8 = r[:8], w[:8]
                last_sum = energy(w, east, lower, diagonal + edge)
                for j, product in enumerate((r8 * r8, r8 * w8, w8 * w8, last_sum)):
                    moments[j, s] = fold(product)
                for e in range(per):
                    pick = picks[e] * weight
                    for j, field in enumerate((v, r, w)):
                        spots[e, j, s] = pick * field[:8, :128]
                    spots[e, 3, s] = empty
            at = pl.ds(pl.multiple_of(k * 8, 8), 8)
            order = [(j, s) for j in range(4) for s in range(sources)]
            sums[0, at, :] = stack_sums([moments[o] for o in order])
            for e in range(per):
                sums[1 + e, at, :] = stack_sums([spots[(e, *o)] for o in order])
        return carry

    lax.fori_loop(0, chunks, forward, 0)
    mark = 3 * sources
    for e in range(per):
        first_cell = (row8 == mark) & (lane8 == 0)
        sums[1 + e, 0:8, :] = sums[1 + e, 0:8, :] + jnp.where(first_cell, elec_ref[e].astype(F32), 0.0)
    for g in range(1 + per):
        pay[g : g + 1, :] = row_sums(sums[g])[0:1, :]

    def spread(src, dst, send, recv, j):
        return pltpu.make_async_remote_copy(
            src_ref=src, dst_ref=dst.at[me], send_sem=send.at[j], recv_sem=recv.at[j],
            device_id={"col": lax.rem(me + j, n)}, device_id_type=MESH,
        )

    def collect(src, dst, send, recv, j):
        return pltpu.make_async_remote_copy(
            src_ref=src, dst_ref=dst.at[lax.rem(me + n - j, n)], send_sem=send.at[j], recv_sem=recv.at[j],
            device_id={"col": lax.rem(me + j, n)}, device_id_type=MESH,
        )

    def start_all(src, dst, send, recv):
        def body(j, carry):
            spread(src, dst, send, recv, j).start()
            return carry

        lax.fori_loop(1, n, body, 0, unroll=n <= 16)
        dst[me] = src[...]

    def wait_all(src, dst, send, recv):
        def body(j, carry):
            collect(src, dst, send, recv, j).wait_recv()
            return carry

        lax.fori_loop(1, n, body, 0, unroll=n <= 16)

    def sent_all(src, dst, send, recv):
        def body(j, carry):
            spread(src, dst, send, recv, j).wait_send()
            return carry

        lax.fori_loop(1, n, body, 0, unroll=n <= 16)

    start_all(pay, got, send1, recv1)

    half = depth // 2

    def before(g, carry):
        arrived(prior_halo(g))
        for step in range(GROUP):
            k = g * GROUP + step
            q = wav_ref[k] * wav_ref[k]
            diagonal = q * c + bottom
            moments = {}
            for s in range(sources):
                ks = k * sources + s
                high = outer(land_ar[ks], land_al[ks])
                prior[ks, 8:16, :] = high
                v = jnp.concatenate([prior[ks, 0:8, :], high], axis=0)
                r = clip(-(divergence(v, east, lower) + diagonal * v))
                w = clip(divergence(r, east, lower) + diagonal * r)
                nu[ks] = r
                nau[ks] = w
                r8, w8 = r[:8, half:], w[:8, half:]
                last_sum = energy(w, east, lower, diagonal + edge)[:, half:]
                for j, product in enumerate((r8 * r8, r8 * w8, w8 * w8, last_sum)):
                    moments[j, s] = product
            at = pl.ds(pl.multiple_of(k * 8, 8), 8)
            sums[0, at, :] = stack_sums([moments[j, s] for j in range(4) for s in range(sources)])
        return carry

    lax.fori_loop(0, chunks, before, 0)

    def spread_weights(row, slot):
        ks = lax.broadcasted_iota(jnp.int32, (fields, 128), 0)
        lanes = lax.broadcasted_iota(jnp.int32, (fields, 128), 1)
        at = lanes == lax.div(ks, sources) * 8 + lax.rem(ks, sources)
        column = jnp.sum(jnp.where(at, jnp.broadcast_to(row, (fields, 128)), 0.0), axis=1, keepdims=True)
        coef[slot] = jnp.broadcast_to(column, (fields, depth))

    wait_all(pay, got, send1, recv1)
    m = jnp.sum(got[:, 0, :], axis=0, keepdims=True)
    first, second = step_weights(m, sources)
    lane = lax.broadcasted_iota(jnp.int32, (1, 128), 1)
    part = lax.div(lax.rem(lane, 8), sources)
    scale = jnp.where(
        part == 0,
        1.0,
        jnp.where(
            part == 1,
            pltpu.roll(first, sources, 1),
            jnp.where(part == 2, pltpu.roll(second, 2 * sources, 1), 0.0),
        ),
    )
    device_ids = lax.broadcasted_iota(jnp.int32, (n, total_e), 0)
    receivers = lax.broadcasted_iota(jnp.int32, (n, total_e), 1)
    marks = [got[:, 1 + e, :] for e in range(per)]
    lane_n = lax.broadcasted_iota(jnp.int32, (n, 128), 1)
    places = [jnp.sum(jnp.where(lane_n == mark, marks[e], 0.0), axis=1, keepdims=True) for e in range(per)]
    columns_here = lax.broadcasted_iota(jnp.int32, (n, 128), 1)
    column_of = (me * cols + jnp.where(columns_here < 8 + RIGHT, columns_here, columns_here - 16)).astype(F32)
    hits = [places[e] == column_of for e in range(per)]
    charges = []
    for s in range(sources):
        scale_s = jnp.where(lax.rem(lane, sources) == s, scale, 0.0)
        pair = []
        row = jnp.zeros((1, total_e), F32)
        for e in range(per):
            potential = jnp.sum(marks[e] * scale_s, axis=1, keepdims=True)
            own_id = device_ids * per + e
            near = jnp.where(receivers == own_id, 1.0, 0.0)
            far = jnp.where(jnp.broadcast_to(far_ref[s : s + 1, :], (n, total_e)) == own_id, 1.0, 0.0)
            pair.append(near - far)
            row = row + jnp.sum(potential * (near - far), axis=0, keepdims=True)
        pred_ref[s : s + 1, :] = row
        misfit = row - obs_ref[s : s + 1, :]
        spots = jnp.zeros((1, 128), F32)
        for e in range(per):
            charge = jnp.sum(pair[e] * misfit, axis=1, keepdims=True)
            spots = spots + jnp.sum(jnp.where(hits[e], charge, 0.0), axis=0, keepdims=True)
        charges.append(spots)

    row16 = lax.broadcasted_iota(jnp.int32, (16, 128), 0)
    lane16 = lax.broadcasted_iota(jnp.int32, (16, 128), 1)
    inside0 = inside[:, :128]
    c0 = c[:, :128]
    east0 = east[:, :128]
    lower0 = jnp.where(lane16 < 127, lower[:, :128], 0.0)
    impulse = []
    for s in range(sources):
        column = jnp.sum(
            jnp.where(lane16 == row16, jnp.broadcast_to(charges[s], (16, 128)), 0.0), axis=1, keepdims=True
        )
        g = jnp.where(lane16 == 0, column, 0.0) * inside0
        b = divergence(g, east0, lower0) * inside0
        d = c0 * g
        impulse.append((g, b, c0 * g))

    def after(g, carry):
        for step in range(GROUP):
            k = g * GROUP + step
            q = wav_ref[k] * wav_ref[k]
            weight = quad_ref[k]
            diagonal = q * c + bottom + edge
            moments = {}
            for s in range(sources):
                ks = k * sources + s
                point, b, d = impulse[s]
                r = weight * point + nu[ks, :, 0:128]
                w = weight * (b + q * d) + nau[ks, :, 0:128]
                nu[ks, :, 0:128] = r
                nau[ks, :, 0:128] = w
                r8, w8 = r[:8], w[:8]
                whole = jnp.concatenate([w, nau[ks, :, half:]], axis=1)
                last_sum = energy(whole, east, lower, diagonal)[:, :128]
                for j, product in enumerate((r8 * r8, r8 * w8, w8 * w8, last_sum)):
                    moments[j, s] = product
            at = pl.ds(pl.multiple_of(k * 8, 8), 8)
            sums[0, at, :] = sums[0, at, :] + stack_sums([moments[j, s] for j in range(4) for s in range(sources)])
        return carry

    lax.fori_loop(0, chunks, after, 0)
    pay2[...] = row_sums(sums[0])[0:1, :]
    start_all(pay2, got2, send2, recv2)

    spread_weights(first, 0)
    spread_weights(second, 1)

    def totals(g, carry):
        for step in range(span):
            ks = g * span + step
            prim[ks] = prim[ks] + coef[0, pl.ds(ks, 1), :] * r0f[ks] + coef[1, pl.ds(ks, 1), :] * w0f[ks]
        return carry

    lax.fori_loop(0, chunks, totals, 0)
    sent_all(pay, got, send1, recv1)
    sent(sigma_halo())
    for g in range(chunks):
        sent(prim_halo(g))
        sent(prior_halo(g))

    wait_all(pay2, got2, send2, recv2)
    first, second = step_weights(jnp.sum(got2[:, 0, :], axis=0, keepdims=True), sources)
    spread_weights(first, 0)
    spread_weights(second, 1)
    last = lax.broadcasted_iota(jnp.int32, (8, depth), 1) == depth - 1

    def correlate(g, total):
        for step in range(GROUP):
            k = g * GROUP + step
            q = wav_ref[k] * wav_ref[k]
            for s in range(sources):
                ks = k * sources + s
                t = prim[ks]
                a = prior[ks] + coef[0, pl.ds(ks, 1), :] * nu[ks] + coef[1, pl.ds(ks, 1), :] * nau[ks]
                t_east, a_east = east_of(t)[:8], east_of(a)[:8]
                t, a = t[:8], a[:8]
                t_down = jnp.where(last, 0.0, pltpu.roll(t, depth - 1, 1))
                a_down = jnp.where(last, 0.0, pltpu.roll(a, depth - 1, 1))
                total = total + ((a_east - a) * (t_east - t) + (a_down - a) * (t_down - t) + q * a * t)
        return total

    grad_ref[...] = lax.fori_loop(0, chunks, correlate, jnp.zeros((8, depth), F32))
    sent_all(pay2, got2, send2, recv2)


def on_device(n, primary, conductivity, wavenumbers, quadrature, electrodes, far_pole, observed, prior_adjoint):
    waves, sources, cols, depth = primary.shape
    fields = waves * sources
    per = electrodes.shape[0]
    vmem = pl.BlockSpec(memory_space=pltpu.VMEM)
    anywhere = pl.BlockSpec(memory_space=pl.ANY)
    wide = pltpu.VMEM((fields, 16, depth), F32)

    def edges(count):
        return pltpu.VMEM((fields, count, depth), F32)

    def sigma_edges(count):
        return pltpu.VMEM((count, depth), F32)

    dma = pltpu.SemaphoreType.DMA
    halos = 2 * (waves // GROUP) + 1
    return pl.pallas_call(
        functools.partial(kernel, n),
        out_shape=(
            jax.ShapeDtypeStruct(observed.shape, F32),
            jax.ShapeDtypeStruct(conductivity.shape, F32),
        ),
        in_specs=[anywhere] * 8,
        out_specs=(vmem, vmem),
        scratch_shapes=[
            wide, wide, pltpu.VMEM((16, depth), F32),
            pltpu.SMEM((waves,), F32), pltpu.SMEM((waves,), F32), pltpu.SMEM((per,), jnp.int32),
            pltpu.VMEM(far_pole.shape, jnp.int32), pltpu.VMEM(observed.shape, F32),
            wide, wide, wide, wide,
            pltpu.VMEM((1 + per, 128, 128), F32),
            pltpu.VMEM((1 + per, 128), F32), pltpu.VMEM((n, 1 + per, 128), F32),
            pltpu.VMEM((1, 128), F32), pltpu.VMEM((n, 1, 128), F32),
            pltpu.VMEM((2, fields, depth), F32),
            dma((8,)), dma((halos,)), dma((halos,)), dma((halos,)), dma((halos,)), dma((n,)), dma((n,)), dma((n,)), dma((n,)),
            edges(LEFT), edges(RIGHT), edges(LEFT), edges(RIGHT), sigma_edges(LEFT), sigma_edges(RIGHT),
            edges(LEFT), edges(RIGHT), edges(LEFT), edges(RIGHT), sigma_edges(LEFT), sigma_edges(RIGHT),
        ],
        compiler_params=pltpu.CompilerParams(
            collective_id=0, has_side_effects=True, vmem_limit_bytes=56 * 1024 * 1024
        ),
    )(
        primary.reshape(fields, cols, depth), conductivity, wavenumbers, quadrature, electrodes, far_pole, observed,
        prior_adjoint.reshape(fields, cols, depth),
    )


def solution(mesh):
    placed = (
        P(None, "lines", "col", None), P("col", "lines"), P(), P(), P(("lines", "col")),
        P("lines", None), P("lines", None), P(None, "lines", "col", None),
    )
    return jax.shard_map(
        functools.partial(on_device, mesh.shape["col"]),
        mesh=mesh, in_specs=placed, out_specs=(P("lines", None), P("col", "lines")), check_vma=False,
    )
```

time: 39.5 us -> 27.2 us (0.69)
  Pallas kernels: 34.1 us -> 23.7 us
  local copies, waits for them, and re-layouts: 4.45 us -> 2.52 us
    pallas_call x1, Pallas kernels: 34.1 us -> 23.7 us  [on_device(): pl.pallas_call(functools.partial(kernel, n), out_shape=(jax.ShapeDtypeStr...]
    unnamed x18 -> x4, local copies, waits for them, and re-layouts: 4.45 us -> 2.52 us
where the time goes in v2:
time: 27.2 us; the launch traced here: 26.9 us
  Pallas kernels  23.7 us (87%)
  local copies, waits for them, and re-layouts  2.52 us (9%)
  between operations  0.65 us (2%)
    pallas_call x1, Pallas kernels, on_device(): pl.pallas_call(functools.partial(kernel, n), out_shape=(jax.ShapeDtypeStr...  23.7 us
    unnamed x4, local copies, waits for them, and re-layouts  2.52 us

profile of v2, /device:TPU:0, one launch (start us, length us, event | category | flops | bytes accessed | tf_op | source)
XLA Modules:
  0.0 26.9 jit_solution(10376129299046751041)
XLA Ops:
  0.6 23.7 %shard_map.95 = (f32[2,32]{1,0:T(2,128)}, f32[8,256]{1,0:T(8,128)}) custom-call(f32[32,8,256]{2,1,0:T(8,128)} %bitcast.2, f32[8,256]{1,0:T(8,128)} %sig_hbm.1, f32[16]{0:T(128)} %wav_hbm.1, f32[16]{0:T(128)} %quad_hbm.1, s32[2]{0:T(128)} %elec_hbm.1, s32[2,32]{1,0:T(2,128)} %far_hbm.1, f32[2,32]{1,0:T(2,128)} %obs_hbm.1, f32[32,8,256]{2,1,0:T(8,128)} %bitcast.3), custom_call_target="tpu_custom_call" | custom-call | tf_op jit(solution)/shard_map/pallas_call | solution.py:469
  24.3 0.0 copy-start
  24.4 0.7 %copy-done = f32[2,32]{1,0:T(2,128)S(1)} copy-done((f32[2,32]{1,0:T(2,128)S(1)}, f32[2,32]{1,0:T(2,128)}, u32[]{:S(2)}) %copy-start) | copy-done | bytes 280
  25.0 0.6 %copy.12 = f32[2,32]{1,0:T(2,128)} copy(f32[2,32]{1,0:T(2,128)S(1)} %copy-done) | data formatting | bytes 512
  25.6 1.3 %copy.13 = f32[8,256]{1,0:T(8,128)} copy(f32[8,256]{1,0:T(8,128)} %get-tuple-element.5) | data formatting | bytes 16384
Async XLA Ops:
  24.3 0.7 %copy-start = (f32[2,32]{1,0:T(2,128)S(1)}, f32[2,32]{1,0:T(2,128)}, u32[]{:S(2)}) copy-start(f32[2,32]{1,0:T(2,128)} %get-tuple-element.4) | copy-start | bytes 772

commit v3 on v2

--- a/solution.py
+++ b/solution.py
@@ -177,8 +177,6 @@
     loads[2].wait()
     pack_ar[...] = prior[:, cols - LEFT : cols, :]
     pack_al[...] = prior[:, 0:RIGHT, :]
-    for g in range(chunks):
-        start_both(prior_halo(g))
     for copy in loads[3:]:
         copy.wait()
 
@@ -288,6 +286,8 @@
         lax.fori_loop(1, n, body, 0, unroll=n <= 16)
 
     start_all(pay, got, send1, recv1)
+    for g in range(chunks):
+        start_both(prior_halo(g))
 
     half = depth // 2
 
@@ -450,6 +450,17 @@
     sent_all(pay2, got2, send2, recv2)
 
 
+def hand_over(pred_in, grad_in, pred_out, grad_out, sem):
+    copies = [
+        pltpu.make_async_copy(pred_in, pred_out, sem.at[0]),
+        pltpu.make_async_copy(grad_in, grad_out, sem.at[1]),
+    ]
+    for copy in copies:
+        copy.start()
+    for copy in copies:
+        copy.wait()
+
+
 def on_device(n, primary, conductivity, wavenumbers, quadrature, electrodes, far_pole, observed, prior_adjoint):
     waves, sources, cols, depth = primary.shape
     fields = waves * sources
@@ -466,7 +477,7 @@
 
     dma = pltpu.SemaphoreType.DMA
     halos = 2 * (waves // GROUP) + 1
-    return pl.pallas_call(
+    results = pl.pallas_call(
         functools.partial(kernel, n),
         out_shape=(
             jax.ShapeDtypeStruct(observed.shape, F32),
@@ -494,6 +505,13 @@
         primary.reshape(fields, cols, depth), conductivity, wavenumbers, quadrature, electrodes, far_pole, observed,
         prior_adjoint.reshape(fields, cols, depth),
     )
+    return pl.pallas_call(
+        hand_over,
+        out_shape=tuple(jax.ShapeDtypeStruct(r.shape, F32) for r in results),
+        in_specs=[anywhere] * 2,
+        out_specs=(anywhere, anywhere),
+        scratch_shapes=[dma((2,))],
+    )(*results)
 
 
 def solution(mesh):

time: 27.2 us -> 24.7 us (0.908)
  local copies, waits for them, and re-layouts: 2.52 us -> 0 us
    unnamed x4 -> x0, local copies, waits for them, and re-layouts: 2.52 us -> none
    pallas_call x0 -> x1, Pallas kernels: none -> 1.4 us  [on_device(): pl.pallas_call(hand_over, out_shape=tuple((jax.ShapeDtypeStruct(r.shape,...]
    pallas_call x1, Pallas kernels: 23.7 us -> 22.4 us  [on_device(): pl.pallas_call(functools.partial(kernel, n), out_shape=(jax.ShapeDtypeStr...]
where the time goes in v3:
time: 24.7 us; the launch traced here: 24.5 us
  Pallas kernels  23.8 us (96%)
  between operations  0.64 us (3%)
    pallas_call x1, Pallas kernels, on_device(): pl.pallas_call(functools.partial(kernel, n), out_shape=(jax.ShapeDtypeStr...  22.4 us
    pallas_call x1, Pallas kernels, on_device(): pl.pallas_call(hand_over, out_shape=tuple((jax.ShapeDtypeStruct(r.shape,...  1.4 us

profile of v3, /device:TPU:0, one launch (start us, length us, event | category | flops | bytes accessed | tf_op | source)
XLA Modules:
  0.0 24.5 jit_solution(16677710604642827890)
XLA Ops:
  0.6 22.4 %shard_map.95 = (f32[2,32]{1,0:T(2,128)}, f32[8,256]{1,0:T(8,128)}) custom-call(f32[32,8,256]{2,1,0:T(8,128)} %bitcast.2, f32[8,256]{1,0:T(8,128)} %sig_hbm.1, f32[16]{0:T(128)} %wav_hbm.1, f32[16]{0:T(128)} %quad_hbm.1, s32[2]{0:T(128)} %elec_hbm.1, s32[2,32]{1,0:T(2,128)} %far_hbm.1, f32[2,32]{1,0:T(2,128)} %obs_hbm.1, f32[32,8,256]{2,1,0:T(8,128)} %bitcast.3), custom_call_target="tpu_custom_call" | custom-call | tf_op jit(solution)/shard_map/pallas_call | solution.py:480
  23.1 1.4 %shard_map.96 = (f32[2,32]{1,0:T(2,128)}, f32[8,256]{1,0:T(8,128)}) custom-call(f32[2,32]{1,0:T(2,128)} %get-tuple-element.4.pred_in, f32[8,256]{1,0:T(8,128)} %get-tuple-element.5.grad_in), custom_call_target="tpu_custom_call" | custom-call | tf_op jit(solution)/shard_map/pallas_call | solution.py:508
